TPU v7x, 32 devices: a whole 2x2x4 slice. The times are simulated.
32 devices in a mesh: cell: 8 (over z, y), dp: 4 (over x, core).
Axes of the slice: x: 2, y: 2, z: 4, core: 2. Of those that a mesh axis runs over, the one named last changes fastest.
Arguments:
- state: bfloat16 [163840, 128], P(('cell', 'dp')), may hold values from -6 to 6
- cell_coordinate: bfloat16 [3, 163840], P(None, ('cell', 'dp')), may hold values from 0 to 1
- member_predictions: bfloat16 [4, 1024, 128], P('dp', 'cell'), may hold values from -6 to 6
- measured_values: float32 [4, 1024], P('dp', 'cell'), may hold values from -64 to 64
- obs_error_variance: float32 [4, 1024], P('dp', 'cell'), may hold values from 4 to 64
- observation_coordinate: bfloat16 [4, 3, 1024], P('dp', None, 'cell'), may hold values from 0 to 1
- localization_tile_pairs: int32 [32, 4, 2, 256], P(('cell', 'dp')), may hold values from 0 to 39, as said below
- used_pair_count: int32 [32, 4], P(('cell', 'dp')), may hold values from 1 to 256, as said below
Outputs:
- analysis: bfloat16 [163840, 128], P(('cell', 'dp'))
Inputs may be any that keep to these rules, and one draw needn't show every extreme that they name: `localization_tile_pairs`: row 0 names a cell tile of the block (below 40), row 1 an observation tile of the batch (below 8); only the first used_pair_count entries count, and a pair may repeat. `used_pair_count`: in every batch some blocks list exactly 256 pairs.
All inputs are finite; a program needn't handle non-finite values.
Results may differ from a plain program's by a relative error of at most 0.011.
Values may be sent and summed in bfloat16 or wider, within the bound.
No kernel may reach another device: no remote copies, remote signals or barrier semaphores. Data moves between devices by JAX's collectives and lax.ppermute only.
A program may use at most 192 MiB of HBM per device.

v0:
```python
import jax
import jax.numpy as jnp
from jax import lax
from jax.sharding import PartitionSpec as P

CT = 128
OBS_DEV = 128


taper_rate = 2.0


def passed_along(block, axis, distance):
    devices = range(lax.axis_size(axis))
    route = [(i - distance, i) for i in devices if i - distance in devices]
    return lax.ppermute(block, axis, route)


def batch_terms(rows, here, obs_tiles, spread, member_pull, obs_places):
    members = spread.shape[1]
    count_tiles = spread.shape[0] // OBS_DEV
    obs_rows = spread.reshape(count_tiles, OBS_DEV, members)[obs_tiles]
    pull_rows = member_pull.reshape(count_tiles, OBS_DEV, members)[obs_tiles]
    obs_here = obs_places.reshape(3, count_tiles, OBS_DEV)[:, obs_tiles]
    dist = jnp.zeros((rows.shape[0], rows.shape[1], OBS_DEV), jnp.float32)
    for axis_pos in range(3):
        diff = here[axis_pos][:, :, None].astype(jnp.float32) - obs_here[axis_pos][
            :, None, :
        ].astype(jnp.float32)
        dist = dist + diff * diff
    score = jnp.einsum("pcm,pom->pco", rows, obs_rows, preferred_element_type=jnp.float32)
    weights = (jnp.exp(-taper_rate * dist) * score).astype(jnp.bfloat16)
    return jnp.einsum("pco,pom->pcm", weights, pull_rows, preferred_element_type=jnp.float32)


def analysis_step(prior_ensemble, value_entries, spread_variance, running_total):
    top_precision = lax.Precision.HIGHEST
    members = running_total.shape[0]
    eye = jnp.eye(members, dtype=jnp.float32)
    present_state = jnp.dot(
        prior_ensemble.astype(jnp.float32), running_total, precision=top_precision
    )
    obs_mean = jnp.mean(present_state, axis=1, keepdims=True)
    spread = present_state - obs_mean
    innovation = value_entries - obs_mean[:, 0]
    inv_var = 1.0 / spread_variance
    local_cross = lax.dot_general(
        spread, spread * inv_var[:, None], (((0,), (0,)), ((), ())), precision=top_precision
    ) / (members - 1)
    local_pull = jnp.dot(inv_var * innovation, spread, precision=top_precision) / (members - 1)
    cross, pull = lax.psum((local_cross, local_pull), "cell")
    chol = jnp.linalg.cholesky(eye + cross)
    inverse = jax.scipy.linalg.cho_solve((chol, True), eye)
    change = jnp.dot(inverse, pull[:, None] - 0.5 * cross, precision=top_precision)
    transform = eye + change - jnp.mean(change, axis=0, keepdims=True)
    member_pull = (inv_var[:, None] * (innovation[:, None] - 0.5 * spread)).astype(jnp.bfloat16)
    return (spread.astype(jnp.bfloat16), member_pull, inverse / (members - 1), transform)


def cell_update(work, places, pairs, count, spread, member_pull, obs_places, inverse):
    members = work.shape[1]
    tiles = work.shape[0] // CT
    slots = pairs.shape[1]
    perturbation = work - jnp.mean(work, axis=1, keepdims=True)
    gain = jnp.dot(perturbation, inverse, precision=lax.Precision.HIGHEST).astype(jnp.bfloat16)
    gain_tiles = gain.reshape(tiles, CT, members)
    place_tiles = places.reshape(3, tiles, CT)
    valid = jnp.arange(slots, dtype=jnp.int32) < count
    cell_tiles = pairs[0]
    rows = gain_tiles[cell_tiles]
    here = place_tiles[:, cell_tiles]
    terms = batch_terms(rows, here, pairs[1], spread, member_pull, obs_places)
    onehot = (
        (cell_tiles[None, :] == jnp.arange(tiles, dtype=jnp.int32)[:, None]) & valid[None, :]
    ).astype(jnp.float32)
    delta = jnp.einsum("tp,pcm->tcm", onehot, terms, precision=lax.Precision.HIGHEST).reshape(
        work.shape
    )
    return work + delta


def local(
    state,
    cell_coordinate,
    member_predictions,
    measured_values,
    obs_error_variance,
    observation_coordinate,
    localization_tile_pairs,
    used_pair_count,
):
    batches = lax.axis_size("dp")
    here_dp = lax.axis_index("dp")
    members = state.shape[1]
    work = state.astype(jnp.float32)
    pair_lists = localization_tile_pairs[0]
    counts = used_pair_count[0]
    running_total = jnp.eye(members, dtype=jnp.float32)
    for step in range(batches):
        spread, member_pull, inverse, transform = analysis_step(
            member_predictions[0], measured_values[0], obs_error_variance[0], running_total
        )
        if step + 1 < batches:
            moved = passed_along(
                jnp.dot(running_total, transform, precision=lax.Precision.HIGHEST), "dp", 1
            )
            running_total = jnp.where(here_dp == step + 1, moved, running_total)
    stacked = (
        lax.all_gather(spread[None], "dp", axis=0, tiled=True),
        lax.all_gather(member_pull[None], "dp", axis=0, tiled=True),
        lax.all_gather(observation_coordinate, "dp", axis=0, tiled=True),
    )
    spread_all, pull_all, places_all = (
        lax.all_gather(stacked[0], "cell", axis=1, tiled=True),
        lax.all_gather(stacked[1], "cell", axis=1, tiled=True),
        lax.all_gather(stacked[2], "cell", axis=2, tiled=True),
    )
    factors = lax.all_gather(inverse[None], "dp", axis=0, tiled=True)
    for batch in range(batches):
        work = cell_update(
            work,
            cell_coordinate,
            pair_lists[batch],
            counts[batch],
            spread_all[batch],
            pull_all[batch],
            places_all[batch],
            factors[batch],
        )
    return work.astype(jnp.bfloat16)


def solution(mesh):
    placed = (
        P(("cell", "dp"), None),
        P(None, ("cell", "dp")),
        P("dp", "cell", None),
        P("dp", "cell"),
        P("dp", "cell"),
        P("dp", None, "cell"),
        P(("cell", "dp"), None, None, None),
        P(("cell", "dp"), None),
    )
    return jax.shard_map(
        local, mesh=mesh, in_specs=placed, out_specs=P(("cell", "dp"), None), check_vma=False
    )
```

profile of v0, /device:TPU:8, one launch (start us, length us, event | category | flops | bytes accessed | tf_op | source)
XLA Modules:
  0.0 786.1 jit_solution(15527878343518646347)
XLA Ops:
  12.1 18.9 %psum.50 = f32[128]{0:T(128)S(1)} all-reduce(f32[128]{0:T(128)S(1)} %fusion.18), channel_id=1, replica_groups=mesh['cell'=8,'dp'=4] {'cell'}, use_global_device_ids=true, to_apply=%region_5.8 | all-reduce | flops 128 | bytes 1024 | tf_op jit(solution)/shard_map/psum | solution.py:51
  38.1 16.4 %all_gather.22 = bf16[4,3,1024]{2,1,0:T(4,128)(2,1)S(1)} all-gather(bf16[4,3,128]{2,1,0:T(4,128)(2,1)S(1)} %all_gather.21), channel_id=1, replica_groups=mesh['cell'=8,'dp'=4] {'cell'}, dimensions={2}, use_global_device_ids=true | all-gather | bytes 27648 | tf_op jit(solution)/shard_map/all_gather | solution.py:116
  65.1 15.6 %all-reduce.5.cloned.1.call-done = f32[128,128]{0,1:T(8,128)} async-done(((f32[128,128]{0,1:T(8,128)}), f32[128,128]{0,1:T(8,128)}) %all-reduce.5.cloned.1.call-update) | async-done | bytes 65552 | tf_op jit(solution)/shard_map/psum | solution.py:51
  82.4 11.7 %cholesky.74 = f32[128,128]{1,0:T(8,128)S(1)} custom-call(f32[128,128]{1,0:T(8,128)S(1)} %fusion.62), custom_call_target="Cholesky" | custom-call | tf_op jit(solution)/shard_map/jit(cholesky)/cholesky | solution.py:52
  112.6 18.0 %psum.52 = f32[128]{0:T(128)S(1)} all-reduce(f32[128]{0:T(128)S(1)} %fusion.17), channel_id=1, replica_groups=mesh['cell'=8,'dp'=4] {'cell'}, use_global_device_ids=true, to_apply=%region_9.12 | all-reduce | flops 128 | bytes 1024 | tf_op jit(solution)/shard_map/psum | solution.py:51
  130.6 52.8 %all-reduce.7.cloned.1.call-done = f32[128,128]{0,1:T(8,128)} async-done(((f32[128,128]{0,1:T(8,128)}), f32[128,128]{0,1:T(8,128)}) %all-reduce.7.cloned.1.call-update) | async-done | bytes 65552 | tf_op jit(solution)/shard_map/psum | solution.py:51
  185.2 11.7 %cholesky.85 = f32[128,128]{1,0:T(8,128)S(1)} custom-call(f32[128,128]{1,0:T(8,128)S(1)} %fusion.57), custom_call_target="Cholesky" | custom-call | tf_op jit(solution)/shard_map/jit(cholesky)/cholesky | solution.py:52
  214.7 17.7 %psum.54 = f32[128]{0:T(128)S(1)} all-reduce(f32[128]{0:T(128)S(1)} %fusion.16), channel_id=1, replica_groups=mesh['cell'=8,'dp'=4] {'cell'}, use_global_device_ids=true, to_apply=%region_13.16 | all-reduce | flops 128 | bytes 1024 | tf_op jit(solution)/shard_map/psum | solution.py:51
  232.4 53.1 %all-reduce.9.cloned.1.call-done = f32[128,128]{0,1:T(8,128)} async-done(((f32[128,128]{0,1:T(8,128)}), f32[128,128]{0,1:T(8,128)}) %all-reduce.9.cloned.1.call-update) | async-done | bytes 65552 | tf_op jit(solution)/shard_map/psum | solution.py:51
  287.3 11.7 %cholesky.96 = f32[128,128]{1,0:T(8,128)S(1)} custom-call(f32[128,128]{1,0:T(8,128)S(1)} %fusion.52), custom_call_target="Cholesky" | custom-call | tf_op jit(solution)/shard_map/jit(cholesky)/cholesky | solution.py:52
  340.0 48.3 %all-reduce.11.cloned.1.call-done = f32[128,128]{0,1:T(8,128)} async-done(((f32[128,128]{0,1:T(8,128)}), f32[128,128]{0,1:T(8,128)}) %all-reduce.11.cloned.1.call-update) | async-done | bytes 65552 | tf_op jit(solution)/shard_map/psum | solution.py:51
  390.1 11.7 %cholesky.107 = f32[128,128]{1,0:T(8,128)S(1)} custom-call(f32[128,128]{1,0:T(8,128)S(1)} %fusion.48), custom_call_target="Cholesky" | custom-call | tf_op jit(solution)/shard_map/jit(cholesky)/cholesky | solution.py:52
  441.4 29.2 %all-gather.8.cloned.1.call-done = bf16[4,1024,128]{2,1,0:T(8,128)(2,1)} async-done(((bf16[4,128,128]{2,1,0:T(8,128)(2,1)}), bf16[4,1024,128]{2,1,0:T(8,128)(2,1)}) %all-gather.8.cloned.1.call-update) | async-done | bytes 1048592 | tf_op jit(solution)/shard_map/all_gather | solution.py:115
  481.1 17.2 %multiply_convert_fusion.3 = bf16[256,128,128]{2,1,0:T(8,128)(2,1)} fusion(bf16[256,128,128]{2,1,0:T(8,128)(2,1)} %gather_fusion.2, bf16[256,128,128]{2,1,0:T(8,128)(2,1)} %gather_fusion.3, f32[256,128]{1,0:T(8,128)S(1)} %bitcast.304, f32[256,128]{1,0:T(8,128)} %bitcast.325, f32[256,128]{1,0:T(8,128)S(1)} %bitcast.303, f32[256,128]{1,0:T(8,128)} %bitcast.324, ...), kind=kOutput, calls=%fused_computation.31 | convolution fusion | flops 1119879168 | bytes 25952256 | tf_op jit(solution)/shard_map/pcm,pom->pco/dot_general | solution.py:31
  498.3 13.9 %fusion.166 = f32[256,128,128]{2,1,0:T(8,128)} fusion(bf16[256,128,128]{2,1,0:T(8,128)(2,1)} %multiply_convert_fusion.3, bf16[256,128,128]{2,1,0:T(8,128)(2,1)} %gather_fusion.4), kind=kOutput, calls=%fused_computation.295 | convolution fusion | flops 1073741824 | bytes 33554432 | tf_op jit(solution)/shard_map/pco,pom->pcm/dot_general | solution.py:33
  512.2 21.1 %fusion.6 = f32[40,128,128]{2,0,1:T(8,128)S(1)} fusion(f32[256,128,128]{2,1,0:T(8,128)} %fusion.166, s32[256]{0:T(256)S(1)} %bitcast.329, pred[256]{0:T(512)(128)(4,1)S(1)} %copy-done.44), kind=kOutput, calls=%fused_computation.26 | convolution fusion | flops 2013286400 | bytes 19399936 | tf_op jit(solution)/shard_map/tp,pcm->tcm/dot_general | solution.py:76
  563.4 17.6 %multiply_convert_fusion.2 = bf16[256,128,128]{2,1,0:T(8,128)(2,1)} fusion(bf16[256,128,128]{2,1,0:T(8,128)(2,1)} %gather_fusion.7, bf16[256,128,128]{2,1,0:T(8,128)(2,1)} %gather_fusion.8, f32[256,128]{1,0:T(8,128)S(1)} %bitcast.319, f32[256,128]{1,0:T(8,128)S(1)} %bitcast.322, f32[256,128]{1,0:T(8,128)S(1)} %bitcast.318, f32[256,128]{1,0:T(8,128)S(1)} %bitcast.321, ...), kind=kOutput, calls=%fused_computation.30 | convolution fusion | flops 1119879168 | bytes 25952256 | tf_op jit(solution)/shard_map/pcm,pom->pco/dot_general | solution.py:31
  581.0 13.9 %fusion.167 = f32[256,128,128]{2,1,0:T(8,128)} fusion(bf16[256,128,128]{2,1,0:T(8,128)(2,1)} %multiply_convert_fusion.2, bf16[256,128,128]{2,1,0:T(8,128)(2,1)} %gather_fusion.9), kind=kOutput, calls=%fused_computation.296 | convolution fusion | flops 1073741824 | bytes 33554432 | tf_op jit(solution)/shard_map/pco,pom->pcm/dot_general | solution.py:33
  594.9 21.1 %fusion.4 = f32[40,128,128]{2,0,1:T(8,128)S(1)} fusion(f32[256,128,128]{2,1,0:T(8,128)} %fusion.167, s32[256]{0:T(256)S(1)} %bitcast.328, pred[256]{0:T(512)(128)(4,1)S(1)} %copy-done.45), kind=kOutput, calls=%fused_computation.24 | convolution fusion | flops 2013286400 | bytes 19399936 | tf_op jit(solution)/shard_map/tp,pcm->tcm/dot_general | solution.py:76
  646.9 17.5 %multiply_convert_fusion.1 = bf16[256,128,128]{2,1,0:T(8,128)(2,1)} fusion(bf16[256,128,128]{2,1,0:T(8,128)(2,1)} %gather_fusion.12, bf16[256,128,128]{2,1,0:T(8,128)(2,1)} %gather_fusion.13, f32[256,128]{1,0:T(8,128)S(1)} %bitcast.313, f32[256,128]{1,0:T(8,128)S(1)} %bitcast.316, f32[256,128]{1,0:T(8,128)S(1)} %bitcast.312, f32[256,128]{1,0:T(8,128)S(1)} %bitcast.315, ...), kind=kOutput, calls=%fused_computation.29 | convolution fusion | flops 1119879168 | bytes 25952256 | tf_op jit(solution)/shard_map/pcm,pom->pco/dot_general | solution.py:31
  675.9 21.4 %fusion.2 = f32[40,128,128]{2,0,1:T(8,128)S(1)} fusion(f32[256,128,128]{2,1,0:T(8,128)} %fusion.168, s32[256]{0:T(256)S(1)} %bitcast.327, pred[256]{0:T(512)(128)(4,1)S(1)} %copy-done.46), kind=kOutput, calls=%fused_computation.22 | convolution fusion | flops 2013286400 | bytes 19399936 | tf_op jit(solution)/shard_map/tp,pcm->tcm/dot_general | solution.py:76
  727.1 17.5 %multiply_convert_fusion = bf16[256,128,128]{2,1,0:T(8,128)(2,1)} fusion(bf16[256,128,128]{2,1,0:T(8,128)(2,1)} %gather_fusion.17, bf16[256,128,128]{2,1,0:T(8,128)(2,1)} %gather_fusion.18, f32[256,128]{1,0:T(8,128)S(1)} %bitcast.307, f32[256,128]{1,0:T(8,128)S(1)} %bitcast.310, f32[256,128]{1,0:T(8,128)S(1)} %bitcast.306, f32[256,128]{1,0:T(8,128)S(1)} %bitcast.309, ...), kind=kOutput, calls=%fused_computation.28 | convolution fusion | flops 1119879168 | bytes 25952256 | tf_op jit(solution)/shard_map/pcm,pom->pco/dot_general | solution.py:31
  744.6 11.5 %fusion.169 = f32[256,128,128]{2,1,0:T(8,128)} fusion(bf16[256,128,128]{2,1,0:T(8,128)(2,1)} %multiply_convert_fusion, bf16[256,128,128]{2,1,0:T(8,128)(2,1)S(1)} %copy-done.5), kind=kOutput, calls=%fused_computation.298 | convolution fusion | flops 1073741824 | bytes 33554432 | tf_op jit(solution)/shard_map/pco,pom->pcm/dot_general | solution.py:33
  756.1 20.9 %fusion = f32[40,128,128]{2,0,1:T(8,128)S(1)} fusion(f32[256,128,128]{2,1,0:T(8,128)} %fusion.169, s32[256]{0:T(256)S(1)} %bitcast.326, pred[256]{0:T(512)(128)(4,1)S(1)} %copy-done.47), kind=kOutput, calls=%fused_computation.20 | convolution fusion | flops 2013286400 | bytes 19399936 | tf_op jit(solution)/shard_map/tp,pcm->tcm/dot_general | solution.py:76
  (250 shorter events, 261.3 us)
Async XLA Ops:
  6.5 50.0 %copy-start = (bf16[3,5120]{1,0:T(4,128)(2,1)S(1)}, bf16[3,5120]{1,0:T(4,128)(2,1)}, u32[]{:S(2)}) copy-start(bf16[3,5120]{1,0:T(4,128)(2,1)} %param.12) | copy-start | bytes 92164
  6.5 206.1 %copy-start.15 = (bf16[1,128,128]{2,1,0:T(8,128)(2,1)S(1)}, bf16[1,128,128]{2,1,0:T(8,128)(2,1)}, u32[]{:S(2)}) copy-start(bf16[1,128,128]{2,1,0:T(8,128)(2,1)} %param.13) | copy-start | bytes 98308
  6.5 74.1 %all-reduce.5.cloned.1.call-start = ((), (), s32[]{:S(2)}) async-start(), calls=%async_computation | async-start | bytes 131072 | tf_op jit(solution)/shard_map/psum | solution.py:51
  9.1 174.3 %all-reduce.7.cloned.1.call-start = ((), (), s32[]{:S(2)}) async-start(), calls=%async_computation.1 | async-start | bytes 131072 | tf_op jit(solution)/shard_map/psum | solution.py:51
  32.8 25.8 %copy-start.39 = (s32[1024]{0:T(1024)}, s32[1024]{0:T(1024)S(1)}, u32[]{:S(2)}) copy-start(s32[1024]{0:T(1024)S(1)} %pad_clamp_fusion.7) | copy-start | bytes 12292
  56.6 362.8 %copy-start.13 = (bf16[5120,128]{1,0:T(8,128)(2,1)S(1)}, bf16[5120,128]{1,0:T(8,128)(2,1)}, u32[]{:S(2)}) copy-start(bf16[5120,128]{1,0:T(8,128)(2,1)} %param.11) | copy-start | bytes 3932164
  59.6 137.4 %copy-start.38 = (s32[1024]{0:T(1024)}, s32[1024]{0:T(1024)S(1)}, u32[]{:S(2)}) copy-start(s32[1024]{0:T(1024)S(1)} %pad_clamp_fusion.1) | copy-start | bytes 12292
  59.6 21.0 %copy-start.36 = (s32[1024]{0:T(1024)}, s32[1024]{0:T(1024)S(1)}, u32[]{:S(2)}) copy-start(s32[1024]{0:T(1024)S(1)} %pad_clamp_fusion) | copy-start | bytes 12292
  107.3 2.5 collective-permute-start
  111.7 173.7 %all-reduce.9.cloned.1.call-start = ((), (), s32[]{:S(2)}) async-start(), calls=%async_computation.2 | async-start | bytes 131072 | tf_op jit(solution)/shard_map/psum | solution.py:51
  210.1 2.5 collective-permute-start.1
  213.8 174.5 %all-reduce.11.cloned.1.call-start = ((), (), s32[]{:S(2)}) async-start(), calls=%async_computation.3 | async-start | bytes 131072 | tf_op jit(solution)/shard_map/psum | solution.py:51
  312.2 2.4 collective-permute-start.2
  316.6 114.2 %all-gather.6.cloned.1.call-start = ((), (), s32[]{:S(2)}) async-start(), calls=%async_computation.4 | async-start | bytes 1179648 | tf_op jit(solution)/shard_map/all_gather | solution.py:114
  325.4 145.2 %all-gather.8.cloned.1.call-start = ((), (), s32[]{:S(2)}) async-start(), calls=%async_computation.5 | async-start | bytes 1179648 | tf_op jit(solution)/shard_map/all_gather | solution.py:115
  581.0 13.9 %copy-start.45 = (pred[256]{0:T(512)(128)(4,1)S(1)}, pred[256]{0:T(512)(128)(4,1)}, u32[]{:S(2)}) copy-start(pred[256]{0:T(512)(128)(4,1)} %iota_compare_fusion.17) | copy-start | bytes 772
  594.9 21.6 %copy-start.12 = (f32[40,128,128]{2,1,0:T(8,128)S(1)}, f32[40,128,128]{2,1,0:T(8,128)}, u32[]{:S(2)}) copy-start(f32[40,128,128]{2,1,0:T(8,128)} %copy-done.11) | copy-start | bytes 7864324
  594.9 21.6 %copy-start.14 = (bf16[5120,128]{1,0:T(8,128)(2,1)S(1)}, bf16[5120,128]{1,0:T(8,128)(2,1)}, u32[]{:S(2)}) copy-start(bf16[5120,128]{1,0:T(8,128)(2,1)} %param.11) | copy-start | bytes 3932164
  646.9 17.5 %copy-start.4 = (bf16[256,128,128]{2,1,0:T(8,128)(2,1)S(1)}, bf16[256,128,128]{2,1,0:T(8,128)(2,1)}, u32[]{:S(2)}) copy-start(bf16[256,128,128]{2,1,0:T(8,128)(2,1)} %gather_fusion.14) | copy-start | bytes 25165828
  675.9 21.9 %copy-start.7 = (f32[5120,128]{1,0:T(8,128)S(1)}, f32[5120,128]{1,0:T(8,128)}, u32[]{:S(2)}) copy-start(f32[5120,128]{1,0:T(8,128)} %copy-done.6) | copy-start | bytes 7864324
  727.1 17.5 %copy-start.5 = (bf16[256,128,128]{2,1,0:T(8,128)(2,1)S(1)}, bf16[256,128,128]{2,1,0:T(8,128)(2,1)}, u32[]{:S(2)}) copy-start(bf16[256,128,128]{2,1,0:T(8,128)(2,1)} %gather_fusion.19) | copy-start | bytes 25165828
  756.1 21.4 %copy-start.8 = (f32[5120,128]{1,0:T(8,128)S(1)}, f32[5120,128]{1,0:T(8,128)}, u32[]{:S(2)}) copy-start(f32[5120,128]{1,0:T(8,128)} %copy-done.6) | copy-start | bytes 7864324
  756.1 21.5 %copy-start.10 = (f32[40,128,128]{2,1,0:T(8,128)S(1)}, f32[40,128,128]{2,1,0:T(8,128)}, u32[]{:S(2)}) copy-start(f32[40,128,128]{2,1,0:T(8,128)} %copy-done.9) | copy-start | bytes 7864324
  756.1 23.0 %copy-start.1 = (bf16[3,5120]{1,0:T(4,128)(2,1)S(1)}, bf16[3,5120]{1,0:T(4,128)(2,1)}, u32[]{:S(2)}) copy-start(bf16[3,5120]{1,0:T(4,128)(2,1)} %param.12) | copy-start | bytes 92164
  (33 other events, 292.2 us)
Sparse Core Ops, SparseCore 0:
  10.8 69.8 all-reduce.4
  111.8 71.5 all-reduce.6
  213.9 71.5 all-reduce.8
  316.7 71.5 all-reduce.10
  390.3 39.1 all-gather.5
  431.6 38.9 all-gather.7
where the time goes:
time: 800 us; the launch traced here: 786 us
  matrix products  229 us (29%)
  waiting for transfers between devices  199 us (25%)
  local copies, waits for them, and re-layouts  124 us (16%)
  other arithmetic  119 us (15%)
  blocking collectives  96.9 us (12%)
  between operations  14.6 us (2%)
    psum x4, waiting for transfers between devices, analysis_step(): cross, pull = lax.psum((local_cross, local_pull), 'cell')  170 us
    dot_general x4, matrix products, cell_update(): jnp.einsum('tp,pcm->tcm', onehot, terms, precision=lax.Precision.HIGHEST)  84.4 us
    dot_general x4, matrix products, batch_terms(): jnp.einsum('pcm,pom->pco', rows, obs_rows, preferred_element_type=jnp.flo...  69.8 us
    psum x3, blocking collectives, analysis_step(): cross, pull = lax.psum((local_cross, local_pull), 'cell')  54.6 us
    dot_general x4, matrix products, batch_terms(): jnp.einsum('pco,pom->pcm', weights, pull_rows, preferred_element_type=jnp...  50.7 us
    another operation x12, other arithmetic, analysis_step(): chol = jnp.linalg.cholesky(eye + cross)  49.5 us
    another operation x8, other arithmetic, analysis_step(): inverse = jax.scipy.linalg.cho_solve((chol, True), eye)  41.9 us
    gather x4, local copies, waits for them, and re-layouts, cell_update(): rows = gain_tiles[cell_tiles]  35.3 us
  transfers between devices with their start and end apart: 9, of which 5 were waited for; matrix products, arithmetic and copies ran while one was open for 10% of the time, Pallas kernels for 0%

commit v1 on v0

v1 whole, which is shorter than its diff:
```python
import functools
import math

import jax
import jax.numpy as jnp
from jax import lax
from jax.experimental import pallas as pl
from jax.experimental.pallas import tpu as pltpu
from jax.sharding import PartitionSpec as P

CT = 128
OBS_DEV = 128
EXTRA = 16
taper_rate = 2.0
LOG2E = math.log2(math.e)
TOP = lax.Precision.HIGHEST
GROUP = 4
F32 = jnp.float32
BF16 = jnp.bfloat16
VMEM_LIMIT = 56 * 1024 * 1024


def in_vmem():
    return pl.BlockSpec(memory_space=pltpu.VMEM)


def in_smem():
    return pl.BlockSpec(memory_space=pltpu.SMEM)


def split3(x):
    hi = x.astype(BF16).astype(F32)
    mid = (x - hi).astype(BF16).astype(F32)
    return hi, mid, x - hi - mid


def split2(x):
    hi = x.astype(BF16)
    return hi, (x - hi.astype(F32)).astype(BF16)


def mm(a, b):
    return jnp.dot(a, b, precision=TOP, preferred_element_type=F32)


def mm16(a, b):
    return jnp.dot(a, b, preferred_element_type=F32)


def pack_kernel(pred, value, variance, coord, out):
    members = pred.shape[1]
    out[:members, :] = pred[...].astype(F32).T.astype(BF16)
    rows = lax.broadcasted_iota(jnp.int32, (EXTRA, OBS_DEV), 0)
    lines = split3(value[...]) + split3(variance[...])
    place = coord[...].astype(F32)
    lines = lines + tuple(place[j : j + 1] for j in range(3))
    extra = jnp.zeros((EXTRA, OBS_DEV), F32)
    for j, line in enumerate(lines):
        extra = jnp.where(rows == j, line, extra)
    out[members:, :] = extra.astype(BF16)


def pack(pred, value, variance, coord):
    return pl.pallas_call(
        pack_kernel,
        out_shape=jax.ShapeDtypeStruct((pred.shape[1] + EXTRA, pred.shape[0]), BF16),
        in_specs=[in_vmem()] * 4,
        out_specs=in_vmem(),
        name="pack_observations",
    )(pred, value, variance, coord)


def inverse_of(eye, s, both):
    n = s.shape[0]
    bound = jnp.max(jnp.sum(jnp.abs(s), axis=0, keepdims=True))
    scale = 2.0 / (2.0 + bound)
    both[:n] = eye - scale * (eye + s)
    both[n:] = eye

    def more(carry):
        rho, left = carry
        return (rho > 1e-8) & (left > 0)

    def factor(carry):
        rho, left = carry
        new = mm(both[...], both[:n])
        both[:n] = new[:n]
        both[n:] += new[n:]
        return rho * rho, left - 1

    lax.while_loop(more, factor, (bound / (2.0 + bound), jnp.int32(40)))
    return scale * both[n:]


def chain_kernel(blocks, identity, bt_out, mp_out, oc_out, yhl, wz, gs, us, both_ref):
    tiles, batches = blocks.shape[0], blocks.shape[1]
    members = blocks.shape[2] - EXTRA
    count = tiles * OBS_DEV
    eye = identity[...]

    for k in range(batches):
        g = jnp.zeros((members + 8, members), F32)
        for u in range(tiles):
            y = blocks[u, k, :members, :].astype(F32)
            e = blocks[u, k, members:, :].astype(F32)
            value = e[0:1] + e[1:2] + e[2:3]
            variance = e[3:4] + e[4:5] + e[5:6]
            place = e[6:9]
            mean = jnp.mean(y, axis=0, keepdims=True)
            yc = y - mean
            w = 1.0 / variance
            z = (value - mean) * w
            ew = jnp.exp(-taper_rate * jnp.sum(place * place, axis=0, keepdims=True))
            where = pl.ds(u * OBS_DEV, OBS_DEV)
            hi, lo = split2(yc)
            yhl[k, :members, where] = hi
            yhl[k, members:, where] = lo
            wz[k, 0:1, where] = w
            wz[k, 1:2, where] = z
            wz[k, 2:3, where] = ew * (1.0 / (members - 1))
            oc_out[k, u] = jnp.concatenate([place * (2 * taper_rate * LOG2E), jnp.zeros((5, OBS_DEV), F32)], axis=0)
            left = jnp.concatenate([yc * w, jnp.broadcast_to(z, (8, OBS_DEV))], axis=0)
            g = g + lax.dot_general(left, yc, (((1,), (1,)), ((), ())), precision=TOP, preferred_element_type=F32)
        gs[k] = g[:members]
        us[k] = g[members:]

    qt = eye - 1.0 / members
    p = jnp.full((8, members), 1.0 / members, F32)
    for k in range(batches):
        g_k = gs[k]
        inverse = inverse_of(eye, g_k * (1.0 / (members - 1)), both_ref)
        step = mm(us[k], inverse) * (1.0 / (members - 1))
        mt = mm(inverse, qt)
        ht = 0.5 * qt + p[0:1]
        hi, lo = split2(jnp.concatenate([mt, ht], axis=0))
        twice = jnp.concatenate([hi, hi], axis=1)
        for u in range(tiles):
            where = pl.ds(u * OBS_DEV, OBS_DEV)
            both = mm16(twice, yhl[k, :, where]) + mm16(lo, yhl[k, :members, where])
            bt_out[k, u] = (both[:members] * wz[k, 2:3, where]).astype(BF16)
            mp_out[k, u] = (wz[k, 1:2, where] - wz[k, 0:1, where] * both[members:]).T.astype(BF16)
        if k + 1 < batches:
            half = 0.5 * (eye + inverse)
            p = p + mm(step, qt)
            qt = 0.5 * (qt + mt)
            for j in range(k + 1, batches):
                g_j = gs[j]
                us[j] = mm(us[j] - mm(step, g_j), half)
                gs[j] = mm(half, mm(g_j, half))


def chain(blocks):
    tiles, batches = blocks.shape[:2]
    members = blocks.shape[2] - EXTRA
    return pl.pallas_call(
        chain_kernel,
        out_shape=(
            jax.ShapeDtypeStruct((batches, tiles, members, OBS_DEV), BF16),
            jax.ShapeDtypeStruct((batches, tiles, OBS_DEV, members), BF16),
            jax.ShapeDtypeStruct((batches, tiles, 8, OBS_DEV), F32),
        ),
        in_specs=[in_vmem()] * 2,
        out_specs=(in_vmem(),) * 3,
        scratch_shapes=[
            pltpu.VMEM((batches, 2 * members, tiles * OBS_DEV), BF16),
            pltpu.VMEM((batches, 8, tiles * OBS_DEV), F32),
            pltpu.VMEM((batches, members, members), F32),
            pltpu.VMEM((batches, 8, members), F32),
            pltpu.VMEM((2 * members, members), F32),
        ],
        compiler_params=pltpu.CompilerParams(vmem_limit_bytes=VMEM_LIMIT),
        name="serial_transforms",
    )(blocks, jnp.eye(members, dtype=F32))


def cell_kernel(codes, mults, sizes, state, coord, select, bt, mp, oc, out, acc, pert, cb, ec):
    batches, obs_tiles = bt.shape[:2]
    members = state.shape[1]
    tiles = state.shape[0] // CT
    def prepare(t, _):
        where = pl.ds(pl.multiple_of(t * CT, CT), CT)
        acc[t] = state[where, :].astype(F32)
        place = lax.dot_general(
            coord[:, where], select[...], (((0,), (0,)), ((), ())), preferred_element_type=F32
        )
        norm = jnp.zeros((CT, members), F32)
        for j in range(3):
            c = place[:, j * members : (j + 1) * members]
            cb[j, t] = c
            norm = norm + c * c
        ec[t] = jnp.exp(-taper_rate * norm)
        return 0

    lax.fori_loop(0, tiles, prepare, 0)
    acc[tiles] = jnp.zeros((CT, members), F32)
    pert[tiles] = jnp.zeros((CT, members), BF16)
    for j in range(3):
        cb[j, tiles] = jnp.zeros((CT, members), F32)

    for k in range(batches):

        def centre(t, _):
            x = acc[t]
            pert[t] = ((x - jnp.mean(x, axis=1, keepdims=True)) * ec[t]).astype(BF16)
            return 0

        lax.fori_loop(0, tiles, centre, 0)

        def several(i, _):
            for j in range(GROUP):
                code = codes[k, i * GROUP + j]
                t, u = code // obs_tiles, code % obs_tiles
                score = mm16(pert[t], bt[k, u]) * mults[k, i * GROUP + j]
                o = oc[k, u]
                x = cb[0, t] * o[0:1] + cb[1, t] * o[1:2] + cb[2, t] * o[2:3]
                weights = (jnp.exp2(x) * score).astype(BF16)
                acc[t] += mm16(weights, mp[k, u])
            return 0

        lax.fori_loop(0, (sizes[k] + GROUP - 1) // GROUP, several, 0)

    def finish(t, _):
        out[pl.ds(pl.multiple_of(t * CT, CT), CT), :] = acc[t].astype(BF16)
        return 0

    lax.fori_loop(0, tiles, finish, 0)


def cells(codes, mults, sizes, state, coord, bt, mp, oc):
    members = state.shape[1]
    select = (jnp.arange(3 * members)[None, :] // members == jnp.arange(16)[:, None]).astype(BF16)
    tiles = state.shape[0] // CT
    return pl.pallas_call(
        cell_kernel,
        out_shape=jax.ShapeDtypeStruct(state.shape, BF16),
        in_specs=[in_smem()] * 3 + [in_vmem()] * 6,
        out_specs=in_vmem(),
        scratch_shapes=[
            pltpu.VMEM((tiles + 1, CT, members), F32),
            pltpu.VMEM((tiles + 1, CT, members), BF16),
            pltpu.VMEM((3, tiles + 1, CT, members), F32),
            pltpu.VMEM((tiles, CT, members), F32),
        ],
        compiler_params=pltpu.CompilerParams(vmem_limit_bytes=VMEM_LIMIT),
        name="cell_updates",
    )(codes, mults, sizes, state, coord, select, bt, mp, oc)


def distinct_pairs(pairs, counts, tiles, obs_tiles):
    slots = pairs.shape[2]
    position = jnp.arange(slots, dtype=jnp.int32)
    valid = position[None, :] < counts[:, None]
    code = jnp.where(valid, pairs[:, 0] * obs_tiles + pairs[:, 1], tiles * obs_tiles)
    same = code[:, :, None] == code[:, None, :]
    times = jnp.sum(same, axis=2, dtype=jnp.int32)
    earlier = position[None, :] < position[:, None]
    first = valid & ~jnp.any(same & earlier[None], axis=2)
    rank = jnp.sum(first[:, None, :] & (code[:, None, :] < code[:, :, None]), axis=2, dtype=jnp.int32)
    slot = jnp.arange(slots + GROUP, dtype=jnp.int32)
    here = first[:, None, :] & (rank[:, None, :] == slot[None, :, None])
    codes = jnp.sum(jnp.where(here, code[:, None, :], 0), axis=2, dtype=jnp.int32)
    mults = jnp.sum(jnp.where(here, times[:, None, :], 0), axis=2, dtype=jnp.int32)
    codes = jnp.where(mults > 0, codes, tiles * obs_tiles)
    sizes = jnp.sum(first, axis=1, dtype=jnp.int32)
    return codes, mults.astype(F32), sizes


def local(
    state,
    cell_coordinate,
    member_predictions,
    measured_values,
    obs_error_variance,
    observation_coordinate,
    localization_tile_pairs,
    used_pair_count,
):
    obs_tiles = lax.axis_size("cell")
    batches = lax.axis_size("dp")
    tiles = state.shape[0] // CT
    mine = pack(member_predictions[0], measured_values, obs_error_variance, observation_coordinate[0])
    blocks = lax.all_gather(mine, ("cell", "dp"), axis=0)
    blocks = blocks.reshape((obs_tiles, batches) + mine.shape)
    codes, mults, sizes = distinct_pairs(localization_tile_pairs[0], used_pair_count[0], tiles, obs_tiles)
    coord = jnp.concatenate([cell_coordinate, jnp.zeros((13, cell_coordinate.shape[1]), BF16)], axis=0)
    bt, mp, oc = chain(blocks)
    return cells(codes, mults, sizes, state, coord, bt, mp, oc)


def solution(mesh):
    placed = (
        P(("cell", "dp"), None),
        P(None, ("cell", "dp")),
        P("dp", "cell", None),
        P("dp", "cell"),
        P("dp", "cell"),
        P("dp", None, "cell"),
        P(("cell", "dp"), None, None, None),
        P(("cell", "dp"), None),
    )
    return jax.shard_map(
        local, mesh=mesh, in_specs=placed, out_specs=P(("cell", "dp"), None), check_vma=False
    )
```

time: 800 us -> 160 us (0.20); the launches traced: 786 us -> 158 us
  matrix products: 229 us -> 0 us
  waiting for transfers between devices: 199 us -> 39.6 us
  local copies, waits for them, and re-layouts: 124 us -> 2.39 us
  other arithmetic: 119 us -> 14.5 us
  blocking collectives: 96.9 us -> 0 us
  Pallas kernels: 0 us -> 88 us
    dot_general x33 -> x0, matrix products: 227 us -> none  [the longest x4 84.4 us: cell_update(): jnp.einsum('tp,pcm->tcm', onehot, terms, precision=lax.Precision.HIGHEST)]
    psum x4 -> x0, waiting for transfers between devices: 170 us -> none  [analysis_step(): cross, pull = lax.psum((local_cross, local_pull), 'cell')]
    gather x20 -> x0, local copies, waits for them, and re-layouts: 112 us -> none  [the longest x4 35.3 us: cell_update(): rows = gain_tiles[cell_tiles]]
    another operation x20 -> x0, other arithmetic: 91.4 us -> none  [the longest x12 49.5 us: analysis_step(): chol = jnp.linalg.cholesky(eye + cross)]
    pallas_call x0 -> x3, Pallas kernels: none -> 88 us  [the longest x1 68 us: cells(): pl.pallas_call(cell_kernel, out_shape=jax.ShapeDtypeStruct(state.shape, B...]
    psum x3 -> x0, blocking collectives: 54.6 us -> none  [analysis_step(): cross, pull = lax.psum((local_cross, local_pull), 'cell')]
    all_gather x5 -> x0, blocking collectives: 42.3 us -> none  [the longest x1 16.4 us: local(): lax.all_gather(stacked[2], 'cell', axis=2, tiled=True)]
    all_gather x2 -> x1, waiting for transfers between devices: 29.2 us -> 39.6 us  [local(): blocks = lax.all_gather(mine, ('cell', 'dp'), axis=0)]
  transfers between devices with their start and end apart: 9 -> 1, of which waited for: 5 -> 1; matrix products, arithmetic and copies ran while one was open for 10% -> 11% of each run, Pallas kernels for 0% -> 0%
where the time goes in v1:
time: 160 us; the launch traced here: 158 us
  Pallas kernels  88 us (55%)
  waiting for transfers between devices  39.6 us (25%)
  other arithmetic  14.5 us (9%)
  between operations  13.4 us (8%)
  local copies, waits for them, and re-layouts  2.39 us (1%)
    pallas_call x1, Pallas kernels, cells(): pl.pallas_call(cell_kernel, out_shape=jax.ShapeDtypeStruct(state.shape, B...  68 us
    all_gather x1, waiting for transfers between devices, local(): blocks = lax.all_gather(mine, ('cell', 'dp'), axis=0)  39.6 us
    pallas_call x1, Pallas kernels, chain(): pl.pallas_call(chain_kernel, out_shape=(jax.ShapeDtypeStruct((batches, ti...  18.5 us
    reduce_sum x1, other arithmetic, distinct_pairs(): jnp.sum(jnp.where(here, times[:, None, :], 0), axis=2, dtype=jnp.int32)  8.85 us
  transfers between devices with their start and end apart: 1, of which 1 were waited for; matrix products, arithmetic and copies ran while one was open for 11% of the time, Pallas kernels for 0%

profile of v1, /device:TPU:8, one launch (start us, length us, event | category | flops | bytes accessed | tf_op | source)
XLA Modules:
  0.0 157.9 jit_solution(7428128073251595512)
XLA Ops:
  6.5 0.0 all-gather.3.cloned.1.call-start
  6.5 1.5 pack_observations.1
  8.0 0.0 all-gather.3.cloned.1.call-update
  8.0 0.7 copy.14
  8.8 0.7 select_bitcast_fusion
  9.5 0.7 bitcast_select_fusion
  10.2 0.4 fusion.2
  10.6 1.4 convert_reduce_fusion.1
  12.0 0.5 fusion.1
  12.6 8.8 %select_reduce_fusion.1 = (s32[4,260]{0,1:T(8,128)S(1)}, s32[4,260]{0,1:T(8,128)S(1)}) fusion(s32[4,256]{1,0:T(4,128)S(1)} %get-tuple-element.11, s32[4,256]{1,0:T(4,128)S(1)} %get-tuple-element.12, pred[4,256]{1,0:T(4,128)(4,1)S(1)} %get-tuple-element.16, s32[4,256]{1,0:T(4,128)S(1)} %select_bitcast_fusion), kind=kLoop, calls=%fused_computation.3 | loop fusion | flops 1595360 | bytes 21632 | tf_op jit(solution)/shard_map/reduce_sum | solution.py:262
  21.4 0.1 copy.10
  21.5 0.1 copy.11
  21.6 1.5 concatenate.3.coord
  23.1 0.6 fusion.3.identity
  23.7 0.6 fusion.4.select
  24.3 0.6 fusion.10
  24.9 39.6 %all-gather.3.cloned.1.call-done = bf16[4608,128]{1,0:T(8,128)(2,1)} async-done(((bf16[144,128]{1,0:T(8,128)(2,1)}), bf16[4608,128]{1,0:T(8,128)(2,1)}) %all-gather.3.cloned.1.call-update) | async-done | bytes 1179664 | tf_op jit(solution)/shard_map/all_gather | solution.py:282
  64.6 18.5 %serial_transforms.1 = (bf16[4,8,128,128]{3,2,1,0:T(8,128)(2,1)}, bf16[4,8,128,128]{3,2,1,0:T(8,128)(2,1)}, f32[4,8,8,128]{3,2,1,0:T(8,128)}) custom-call(bf16[8,4,144,128]{3,2,1,0:T(8,128)(2,1)} %bitcast.11, f32[128,128]{1,0:T(8,128)} %fusion.3.identity), custom_call_target="tpu_custom_call" | custom-call | tf_op jit(solution)/shard_map/serial_transforms/pallas_call | solution.py:155
  83.1 68.0 %cell_updates.1 = bf16[5120,128]{1,0:T(8,128)(2,1)} custom-call(s32[4,260]{1,0:T(4,128)} %get-tuple-element.18.codes, f32[4,260]{1,0:T(4,128)} %get-tuple-element.17.mults, s32[4]{0:T(128)} %get-tuple-element.15.sizes, bf16[5120,128]{1,0:T(8,128)(2,1)} %state.1, bf16[16,5120]{1,0:T(8,128)(2,1)} %concatenate.3.coord, bf16[16,384]{1,0:T(8,128)(2,1)} %fusion.4.select, ...), custom_call_target="tpu_custom_call" | custom-call | tf_op jit(solution)/shard_map/cell_updates/pallas_call | solution.py:233
  (2 shorter events, 0.0 us)
Async XLA Ops:
  6.5 58.0 %all-gather.3.cloned.1.call-start = ((), (), s32[]{:S(2)}) async-start(), calls=%async_computation | async-start | bytes 1216512 | tf_op jit(solution)/shard_map/all_gather | solution.py:282
Sparse Core Ops, SparseCore 0:
  10.3 54.2 all-gather.2
